TPU v7x, 32 devices: a whole 2x2x4 slice. The times are simulated.
32 devices in a mesh: dom: 8 (over z, y), group: 4 (over x, core).
Axes of the slice: x: 2, y: 2, z: 4, core: 2. Of those that a mesh axis runs over, the one named last changes fastest.
Arguments:
- embeddings: float32 [8192, 400], P(('dom', 'group')), may hold values from -3 to 3
- adagrad_state: float32 [8192], P(('dom', 'group')), may hold values from 0.05 to 0.5
- relation_diag: float32 [64, 400], replicated, may hold values from 0.1 to 1.9
- bucket_counts: int32 [2, 8], P(None, 'dom'), may hold values from 512 to 4096, as said below
- src_index: int32 [2, 8, 4096], P(None, 'dom', 'group'), may hold values from 0 to 1023
- dst_index: int32 [2, 8, 4096], P(None, 'dom', 'group'), may hold values from 0 to 1023
- rel_index: int32 [2, 8, 4096], P(None, 'dom', 'group'), may hold values from 0 to 63
- neg_index: int32 [2, 8, 4, 1024], P(None, 'dom', 'group'), may hold values from 0 to 1023
Outputs:
- new_embeddings: float32 [8192, 400], P(('dom', 'group'))
- new_state: float32 [8192], P(('dom', 'group'))
Inputs may be any that keep to these rules, and one draw needn't show every extreme that they name: bucket_counts holds the live edges of each bucket; live slots are the first ones of the bucket; at least one bucket is full and at least one holds exactly 512 live edges.
All inputs are finite; a program needn't handle non-finite values.
Results may differ from a plain program's by a relative error of at most 0.0016.
Values may be sent and summed in bfloat16 or wider, within the bound.
A program may use at most 64 MiB of HBM per device.

v0:
```python
import jax
import jax.numpy as jnp
from jax import lax
from jax.sharding import PartitionSpec as P

ROUNDS = 2


LEARN_RATE = 0.1
ROW_EPS = 1e-06


def from_behind(block, axis, distance):
    devices = range(lax.axis_size(axis))
    route = [((i - distance) % len(devices), i) for i in devices]
    return lax.ppermute(block, axis, route)


def select_table(row_ids, count):
    return row_ids[:, None] == lax.iota(jnp.int32, count)[None, :]


def pick_rows(table, block):
    return jnp.dot(table.astype(jnp.bfloat16), block, preferred_element_type=jnp.float32).astype(
        jnp.bfloat16
    )


def add_rows(table, values):
    return lax.dot_general(
        table.astype(jnp.float32), values, (((0,), (0,)), ((), ())), precision=lax.Precision.HIGHEST
    )


def block_grads(lhs_block, rhs_block, relation_diag, src_ids, dst_ids, rel_ids, neg_ids, live_mask):
    part_rows = lhs_block.shape[0]
    src_table = select_table(src_ids, part_rows)
    dst_table = select_table(dst_ids, part_rows)
    neg_table = select_table(neg_ids, part_rows)
    lhs_rows = pick_rows(src_table, lhs_block)
    rhs_rows = pick_rows(dst_table, rhs_block)
    neg_rows = pick_rows(neg_table, rhs_block)
    relation_count = relation_diag.shape[0]
    onehot = select_table(rel_ids, relation_count).astype(jnp.float32)
    rel_rows = jnp.dot(onehot, relation_diag, precision=lax.Precision.HIGHEST)
    query_rows = lhs_rows.astype(jnp.float32) * rel_rows
    query_half = query_rows.astype(jnp.bfloat16)
    rhs_wide = rhs_rows.astype(jnp.float32)
    pos_score = jnp.sum(query_rows * rhs_wide, axis=1)
    scores = lax.dot_general(
        query_half, neg_rows, (((1,), (1,)), ((), ())), preferred_element_type=jnp.float32
    )
    weights = (live_mask[:, None] * jax.nn.sigmoid(scores) / neg_ids.shape[0]).astype(jnp.bfloat16)
    pos_coef = -live_mask * jax.nn.sigmoid(-pos_score)
    grad_query = pos_coef[:, None] * rhs_wide + jnp.dot(
        weights, neg_rows, preferred_element_type=jnp.float32
    )
    grad_neg = lax.dot_general(
        weights, query_half, (((0,), (0,)), ((), ())), preferred_element_type=jnp.float32
    )
    lhs_grad = add_rows(src_table, grad_query * rel_rows)
    both_tables = jnp.concatenate([dst_table, neg_table], axis=0)
    both_terms = jnp.concatenate([pos_coef[:, None] * query_rows, grad_neg], axis=0)
    rhs_grad = add_rows(both_tables, both_terms)
    return (lhs_grad, rhs_grad)


def per_device(
    embeddings,
    adagrad_state,
    relation_diag,
    bucket_counts,
    src_index,
    dst_index,
    rel_index,
    neg_index,
):
    emb_half = embeddings.astype(jnp.bfloat16)
    own_block = lax.all_gather(emb_half, "group", axis=0, tiled=True)
    part_rows = own_block.shape[0]
    emb_width = embeddings.shape[1]
    edge_slots = src_index.shape[2]
    slot_ids = lax.axis_index("group") * edge_slots + lax.iota(jnp.int32, edge_slots)
    lhs_partial = jnp.zeros((part_rows, emb_width), jnp.float32)
    for turn_index in range(ROUNDS):
        shift_by = turn_index + 1
        far_quarter = from_behind(emb_half, "dom", shift_by)
        rhs_block = lax.all_gather(far_quarter, "group", axis=0, tiled=True)
        live_mask = (slot_ids < bucket_counts[turn_index, 0]).astype(jnp.float32)
        lhs_grad, rhs_grad = block_grads(
            own_block,
            rhs_block,
            relation_diag,
            src_index[turn_index, 0],
            dst_index[turn_index, 0],
            rel_index[turn_index, 0],
            neg_index[turn_index, 0, 0],
            live_mask,
        )
        lhs_partial = lhs_partial + lhs_grad
        lhs_partial = lhs_partial + from_behind(rhs_grad, "dom", -shift_by)
    grad_total = lax.psum_scatter(lhs_partial, "group", scatter_dimension=0, tiled=True)
    new_state = adagrad_state + jnp.mean(grad_total * grad_total, axis=1)
    new_embeddings = embeddings - LEARN_RATE * grad_total / (jnp.sqrt(new_state)[:, None] + ROW_EPS)
    return (new_embeddings, new_state)


def solution(mesh):
    placed = (
        P(("dom", "group"), None),
        P(("dom", "group")),
        P(),
        P(None, "dom"),
        P(None, "dom", "group"),
        P(None, "dom", "group"),
        P(None, "dom", "group"),
        P(None, "dom", "group", None),
    )
    return jax.shard_map(
        per_device,
        mesh=mesh,
        in_specs=placed,
        out_specs=(P(("dom", "group"), None), P(("dom", "group"))),
        check_vma=False,
    )
```

profile of v0, /device:TPU:0, one launch (start us, length us, event | category | flops | bytes accessed | tf_op | source)
XLA Modules:
  0.0 182.4 jit_solution(4930111839963931823)
XLA Ops:
  7.2 0.0 copy-start
  7.2 0.0 reduce-scatter.2.cloned.1.call-start
  7.3 1.7 convert_element_type.78
  9.0 3.0 %collective-permute-start.2 = (bf16[256,400]{0,1:T(8,128)(2,1)}, bf16[256,400]{0,1:T(8,128)(2,1)}, u32[]{:S(2)}, u32[]{:S(2)}) collective-permute-start(bf16[256,400]{0,1:T(8,128)(2,1)} %convert_element_type.78), channel_id=1, source_target_pairs={{24,0},{28,4},{0,8},{4,12},{8,16},{12,20},{16,24},{20,28},{25,1},{... | collective-permute-start | bytes 614408 | tf_op jit(solution)/shard_map/ppermute | solution.py:16
  12.0 1.5 collective-permute-start
  13.5 9.8 %all_gather.9 = bf16[1024,400]{0,1:T(8,128)(2,1)} all-gather(bf16[256,400]{0,1:T(8,128)(2,1)} %convert_element_type.78), channel_id=1, replica_groups=mesh['dom'=8,'group'=4] {'group'}, dimensions={0}, use_global_device_ids=true | all-gather | bytes 1024000 | tf_op jit(solution)/shard_map/all_gather | solution.py:79
  23.4 0.6 fusion.58
  24.0 0.6 fusion.49
  24.7 0.7 fusion.48
  25.3 0.0 copy-done
  25.3 1.0 fusion.37
  26.4 1.0 fusion.36
  27.4 0.0 copy-start.6
  27.4 1.5 iota_compare_fusion
  28.9 1.5 iota_compare_fusion.5
  30.5 0.0 collective-permute-done.2
  30.5 9.1 %all_gather.11 = bf16[1024,400]{0,1:T(8,128)(2,1)S(1)} all-gather(bf16[256,400]{0,1:T(8,128)(2,1)} %collective-permute-done.2), channel_id=1, replica_groups=mesh['dom'=8,'group'=4] {'group'}, dimensions={0}, use_global_device_ids=true | all-gather | bytes 1024000 | tf_op jit(solution)/shard_map/all_gather | solution.py:88
  39.6 1.3 convolution_convert_fusion
  40.8 1.3 convolution_convert_fusion.1
  42.1 0.0 collective-permute-done
  42.1 9.3 %all_gather.10 = bf16[1024,400]{0,1:T(8,128)(2,1)S(1)} all-gather(bf16[256,400]{0,1:T(8,128)(2,1)} %collective-permute-done), channel_id=1, replica_groups=mesh['dom'=8,'group'=4] {'group'}, dimensions={0}, use_global_device_ids=true | all-gather | bytes 1024000 | tf_op jit(solution)/shard_map/all_gather | solution.py:88
  51.4 1.2 convolution_convert_fusion.2
  52.7 1.2 convolution_convert_fusion.3
  53.9 1.3 fusion.26
  55.3 1.9 %multiply_convert_fusion = bf16[1024,1024]{1,0:T(8,128)(2,1)S(1)} fusion(bf16[1024,400]{0,1:T(8,128)(2,1)S(1)} %convolution_convert_fusion, f32[1024]{0:T(1024)S(1)} %fusion.49, f32[1024,400]{0,1:T(8,128)S(1)} %get-tuple-element.15), kind=kOutput, calls=%fused_computation.8 | convolution fusion | flops 845561856 | bytes 4558848 | tf_op jit(solution)/shard_map/dot_general | solution.py:50
  57.2 1.0 fusion.38
  58.3 0.6 divide_multiply_fusion
  58.9 0.2 broadcast_multiply_fusion
  59.1 5.3 %fusion.4 = f32[1024,400]{0,1:T(8,128)S(1)} fusion(pred[1024,1024]{1,0:T(32,128)(4,1)S(1)} %get-tuple-element.18, pred[1024,1024]{1,0:T(32,128)(4,1)S(1)} %get-tuple-element.19, f32[1024,400]{0,1:T(8,128)S(1)} %fusion.38, f32[1024,400]{0,1:T(8,128)S(1)} %broadcast_multiply_fusion), kind=kOutput, calls=%fused_computation.4 | convolution fusion | flops 10069245952 | bytes 7012352 | tf_op jit(solution)/shard_map/dot_general | solution.py:30
  64.4 2.6 %collective-permute-start.3 = (f32[1024,400]{0,1:T(8,128)S(1)}, f32[1024,400]{0,1:T(8,128)S(1)}, u32[]{:S(2)}, u32[]{:S(2)}) collective-permute-start(f32[1024,400]{0,1:T(8,128)S(1)} %fusion.4), channel_id=1, source_target_pairs={{8,0},{12,4},{16,8},{20,12},{24,16},{28,20},{0,24},{4,28},{9,1},{1... | collective-permute-start | bytes 4915208 | tf_op jit(solution)/shard_map/ppermute | solution.py:16
  67.0 1.3 fusion.22
  68.3 1.9 %multiply_convert_fusion.1 = bf16[1024,1024]{1,0:T(8,128)(2,1)S(1)} fusion(bf16[1024,400]{0,1:T(8,128)(2,1)S(1)} %convolution_convert_fusion.2, f32[1024]{0:T(1024)S(1)} %fusion.48, f32[1024,400]{0,1:T(8,128)S(1)} %get-tuple-element.17), kind=kOutput, calls=%fused_computation.14 | convolution fusion | flops 845561856 | bytes 4558848 | tf_op jit(solution)/shard_map/dot_general | solution.py:50
  70.3 1.0 fusion.41
  71.3 0.7 divide_multiply_fusion.1
  72.0 0.2 broadcast_multiply_fusion.1
  72.2 5.3 %fusion = f32[1024,400]{0,1:T(8,128)S(1)} fusion(pred[1024,1024]{1,0:T(32,128)(4,1)S(1)} %get-tuple-element.20, pred[1024,1024]{1,0:T(32,128)(4,1)S(1)} %get-tuple-element.21, f32[1024,400]{0,1:T(8,128)S(1)} %fusion.41, f32[1024,400]{0,1:T(8,128)S(1)} %broadcast_multiply_fusion.1), kind=kOutput, calls=%fused_computation | convolution fusion | flops 10069245952 | bytes 7012352 | tf_op jit(solution)/shard_map/dot_general | solution.py:30
  77.5 1.8 collective-permute-start.1
  79.3 1.0 fusion.60
  80.3 1.0 fusion.59
  81.4 3.3 %fusion.8 = f32[1024,400]{0,1:T(8,128)S(1)} fusion(s32[1024]{0:T(1024)S(1)} %bitcast.39, f32[1024,400]{0,1:T(8,128)S(1)} %fusion.37, f32[1024,400]{0,1:T(8,128)S(1)} %fusion.60, bf16[1024,400]{0,1:T(8,128)(2,1)S(1)} %convolution_convert_fusion.1, f32[1024]{0:T(1024)S(1)} %divide_multiply_fusion), kind=kOutput, calls=%fused_computation.12 | convolution fusion | flops 5035851776 | bytes 5742592 | tf_op jit(solution)/shard_map/dot_general | solution.py:30
  84.7 18.6 %collective-permute-done.3 = f32[1024,400]{0,1:T(8,128)S(1)} collective-permute-done((f32[1024,400]{0,1:T(8,128)S(1)}, f32[1024,400]{0,1:T(8,128)S(1)}, u32[]{:S(2)}, u32[]{:S(2)}) %collective-permute-start.3) | collective-permute-done | bytes 1638432 | tf_op jit(solution)/shard_map/ppermute | solution.py:16
  103.3 34.4 %collective-permute-done.1 = f32[1024,400]{0,1:T(8,128)S(1)} collective-permute-done((f32[1024,400]{0,1:T(8,128)S(1)}, f32[1024,400]{0,1:T(8,128)S(1)}, u32[]{:S(2)}, u32[]{:S(2)}) %collective-permute-start.1) | collective-permute-done | bytes 1638432 | tf_op jit(solution)/shard_map/ppermute | solution.py:16
  137.7 4.7 %add_add_fusion = f32[1024,400]{0,1:T(8,128)} fusion(f32[1024,400]{0,1:T(8,128)S(1)} %collective-permute-done.3, f32[1024,400]{0,1:T(8,128)S(1)} %fusion.8, f32[1024,400]{0,1:T(8,128)S(1)} %collective-permute-done.1, f32[1024,400]{0,1:T(8,128)S(1)} %fusion.36, f32[1024,400]{0,1:T(8,128)S(1)} %fusion.59, ...), kind=kOutput, calls=%fused_computation.40 | convolution fusion | flops 5037080576 | bytes 10657792 | tf_op jit(solution)/shard_map/dot_general | solution.py:30
  142.4 0.0 reduce-scatter.2.cloned.1.call-update
  142.4 29.7 %reduce-scatter.2.cloned.1.call-done = f32[256,400]{0,1:T(8,128)} async-done(((f32[1024,400]{0,1:T(8,128)}), f32[256,400]{0,1:T(8,128)}) %reduce-scatter.2.cloned.1.call-update) | async-done | bytes 409616 | tf_op jit(solution)/shard_map/reduce_scatter | solution.py:102
  172.1 1.1 multiply_reduce_fusion
  173.2 0.6 sqrt_add_fusion
  173.7 1.8 divide_subtract_fusion
  (19 shorter events, 0.0 us)
Async XLA Ops:
  7.2 18.2 %copy-start = (f32[64,400]{1,0:T(8,128)S(1)}, f32[64,400]{1,0:T(8,128)}, u32[]{:S(2)}) copy-start(f32[64,400]{1,0:T(8,128)} %param.10) | copy-start | bytes 307204
  7.2 16.2 %copy-start.3 = (s32[2,1,1,1024]{3,2,1,0:T(1,128)S(1)}, s32[2,1,1,1024]{3,2,1,0:T(1,128)}, u32[]{:S(2)}) copy-start(s32[2,1,1,1024]{3,2,1,0:T(1,128)} %param.15) | copy-start | bytes 24580
  7.2 16.2 %copy-start.4 = (s32[2,1,1024]{2,1,0:T(1,128)S(1)}, s32[2,1,1024]{2,1,0:T(1,128)}, u32[]{:S(2)}) copy-start(s32[2,1,1024]{2,1,0:T(1,128)} %param.13) | copy-start | bytes 24580
  7.2 16.2 %copy-start.7 = (s32[2,1]{0,1:T(1,128)S(1)}, s32[2,1]{0,1:T(1,128)}, u32[]{:S(2)}) copy-start(s32[2,1]{0,1:T(1,128)} %param.11) | copy-start | bytes 28
  7.2 16.8 %copy-start.5 = (s32[2,1,1024]{2,1,0:T(1,128)S(1)}, s32[2,1,1024]{2,1,0:T(1,128)}, u32[]{:S(2)}) copy-start(s32[2,1,1024]{2,1,0:T(1,128)} %param.14) | copy-start | bytes 24580
  7.2 164.9 %reduce-scatter.2.cloned.1.call-start = ((), (), s32[]{:S(2)}) async-start(), calls=%async_computation.1 | async-start | bytes 2048000 | tf_op jit(solution)/shard_map/reduce_scatter | solution.py:102
  9.0 21.5 %collective-permute-start.2 = (bf16[256,400]{0,1:T(8,128)(2,1)}, bf16[256,400]{0,1:T(8,128)(2,1)}, u32[]{:S(2)}, u32[]{:S(2)}) collective-permute-start(bf16[256,400]{0,1:T(8,128)(2,1)} %convert_element_type.78), channel_id=1, source_target_pairs={{24,0},{28,4},{0,8},{4,12},{8,16},{12,20},{16,24},{20,28},{25,1},{... | collective-permute-start | bytes 614408 | tf_op jit(solution)/shard_map/ppermute | solution.py:16
  12.0 30.1 %collective-permute-start = (bf16[256,400]{0,1:T(8,128)(2,1)}, bf16[256,400]{0,1:T(8,128)(2,1)}, u32[]{:S(2)}, u32[]{:S(2)}) collective-permute-start(bf16[256,400]{0,1:T(8,128)(2,1)} %convert_element_type.78), channel_id=1, source_target_pairs={{28,0},{0,4},{4,8},{8,12},{12,16},{16,20},{20,24},{24,28},{29,1},{... | collective-permute-start | bytes 614408 | tf_op jit(solution)/shard_map/ppermute | solution.py:16
  27.4 3.1 %copy-start.6 = (s32[2,1,1024]{2,1,0:T(1,128)S(1)}, s32[2,1,1024]{2,1,0:T(1,128)}, u32[]{:S(2)}) copy-start(s32[2,1,1024]{2,1,0:T(1,128)} %param.12) | copy-start | bytes 24580
  52.7 1.3 copy-start.2
  64.4 38.9 %collective-permute-start.3 = (f32[1024,400]{0,1:T(8,128)S(1)}, f32[1024,400]{0,1:T(8,128)S(1)}, u32[]{:S(2)}, u32[]{:S(2)}) collective-permute-start(f32[1024,400]{0,1:T(8,128)S(1)} %fusion.4), channel_id=1, source_target_pairs={{8,0},{12,4},{16,8},{20,12},{24,16},{28,20},{0,24},{4,28},{9,1},{1... | collective-permute-start | bytes 4915208 | tf_op jit(solution)/shard_map/ppermute | solution.py:16
  77.5 60.2 %collective-permute-start.1 = (f32[1024,400]{0,1:T(8,128)S(1)}, f32[1024,400]{0,1:T(8,128)S(1)}, u32[]{:S(2)}, u32[]{:S(2)}) collective-permute-start(f32[1024,400]{0,1:T(8,128)S(1)} %fusion), channel_id=1, source_target_pairs={{4,0},{8,4},{12,8},{16,12},{20,16},{24,20},{28,24},{0,28},{5,1},{9... | collective-permute-start | bytes 4915208 | tf_op jit(solution)/shard_map/ppermute | solution.py:16
  142.4 30.8 %copy-start.8 = (f32[256]{0:T(256)S(1)}, f32[256]{0:T(256)}, u32[]{:S(2)}) copy-start(f32[256]{0:T(256)} %param.9) | copy-start | bytes 3076
  142.4 31.3 %copy-start.1 = (f32[256,400]{0,1:T(8,128)S(1)}, f32[256,400]{0,1:T(8,128)}, u32[]{:S(2)}) copy-start(f32[256,400]{0,1:T(8,128)} %param.8) | copy-start | bytes 1228804
Sparse Core Ops, SparseCore 0:
  142.5 29.5 reduce-scatter.1
where the time goes:
time: 183 us; the launch traced here: 182 us
  waiting for transfers between devices  82.7 us (45%)
  matrix products  36.3 us (20%)
  blocking collectives  28.2 us (15%)
  between operations  14.3 us (8%)
  other arithmetic  11.2 us (6%)
  starting transfers between devices  8.97 us (5%)
    ppermute x4, waiting for transfers between devices, from_behind(): return lax.ppermute(block, axis, route)  53 us
    reduce_scatter x1, waiting for transfers between devices, per_device(): lax.psum_scatter(lhs_partial, 'group', scatter_dimension=0, tiled=True)  29.7 us
    dot_general x4, matrix products, add_rows(): lax.dot_general(table.astype(jnp.float32), values, (((0,), (0,)), ((), ()...  18.5 us
    all_gather x2, blocking collectives, per_device(): rhs_block = lax.all_gather(far_quarter, 'group', axis=0, tiled=True)  18.4 us
    all_gather x1, blocking collectives, per_device(): own_block = lax.all_gather(emb_half, 'group', axis=0, tiled=True)  9.83 us
    ppermute x4, starting transfers between devices, from_behind(): return lax.ppermute(block, axis, route)  8.94 us
    dot_general x6, matrix products, pick_rows(): jnp.dot(table.astype(jnp.bfloat16), block, preferred_element_type=jnp.flo...  7.63 us
    dot_general x2, matrix products, block_grads(): lax.dot_general(query_half, neg_rows, (((1,), (1,)), ((), ())), preferred...  3.89 us
  transfers between devices with their start and end apart: 5, of which 3 were waited for; matrix products, arithmetic and copies ran while one was open for 14% of the time, Pallas kernels for 0%

commit v1 on v0

v1 whole, which is shorter than its diff:
```python
import jax
import jax.numpy as jnp
from jax import lax
from jax.experimental import pallas as pl
from jax.experimental.pallas import tpu as pltpu
from jax.sharding import PartitionSpec as P

ROUNDS = 2
LEARN_RATE = 0.1
ROW_EPS = 1e-06
MESH = pl.DeviceIdType.MESH
BF = jnp.bfloat16
F32 = jnp.float32


def dot_nn(a, b):
    return lax.dot_general(a, b, (((1,), (0,)), ((), ())), preferred_element_type=F32)


def dot_nt(a, b):
    return lax.dot_general(a, b, (((1,), (1,)), ((), ())), preferred_element_type=F32)


def dot_tn(a, b):
    return lax.dot_general(a, b, (((0,), (0,)), ((), ())), preferred_element_type=F32)


def logistic(x):
    return 0.5 * jnp.tanh(0.5 * x) + 0.5


def kernel(
    n_dom,
    n_group,
    neg_slots,
    counts_ref,
    emb_ref,
    state_ref,
    rel_ref,
    src_ref,
    dst_ref,
    relid_ref,
    neg_ref,
    out_ref,
    new_state_ref,
    parts,
    src_hot,
    query,
    query_half,
    rel_rows,
    grad_query,
    lhs_sum,
    outbox,
    core_in,
    pair_out,
    pair_in,
    far_out,
    far_in,
    send_sem,
    recv_sem,
):
    w = lax.axis_index("dom")
    g = lax.axis_index("group")
    width, quarter = emb_ref.shape
    edges = src_ref.shape[2]
    core = lax.rem(g, 2)
    core_g = g + 1 - 2 * core
    half_g = lax.rem(g + 2, n_group)
    both_g = lax.rem(core_g + 2, n_group)

    def to(dom, group):
        return (dom, group)

    def dom_at(distance):
        return lax.rem(w + n_dom + distance, n_dom)

    barrier = pltpu.get_barrier_semaphore()
    friends = [(w, core_g), (w, half_g)]
    for k in range(1, ROUNDS + 1):
        friends += [(dom_at(k), g), (dom_at(-k), g)]
    for friend in friends:
        pl.semaphore_signal(barrier, inc=1, device_id=friend, device_id_type=MESH)

    parts[0, g] = emb_ref[...].astype(BF)
    pl.semaphore_wait(barrier, len(friends))

    used = [0]

    def send(src, dst, device):
        i = used[0]
        used[0] += 1
        copy = pltpu.make_async_remote_copy(
            src_ref=src,
            dst_ref=dst,
            send_sem=send_sem.at[i],
            recv_sem=recv_sem.at[i],
            device_id=device,
            device_id_type=MESH,
        )
        copy.start()
        return copy

    pending = []

    def spread(k):
        a = send(parts.at[k, g], parts.at[k, g], (w, half_g))
        b = send(parts.at[k, g], parts.at[k, g], (w, core_g))
        return a, b

    def forward(k, copies):
        copies[0].wait_recv()
        c = send(parts.at[k, half_g], parts.at[k, half_g], (w, core_g))
        pending.extend([copies[0], copies[1], c])
        return copies[1], c

    def arrived(copies):
        for copy in copies:
            copy.wait_recv()

    far = [
        send(parts.at[0, g], parts.at[k, g], (dom_at(k), g)) for k in range(1, ROUNDS + 1)
    ]
    pending.extend(far)
    own = spread(0)

    rel_t = rel_ref[...].T
    rel_hi = rel_t.astype(BF)
    rel_lo = (rel_t - rel_hi.astype(F32)).astype(BF)
    rel_count = rel_t.shape[1]

    def hot(ids, base, rows):
        return lax.broadcasted_iota(jnp.int32, (rows, edges), 0) + base == ids

    def hot_half(ids, base, rows):
        return jnp.where(hot(ids, base, rows), 1.0, 0.0).astype(BF)

    def queries(r):
        total = None
        src_ids = src_ref[r]
        for q in range(n_group):
            table = hot_half(src_ids, q * quarter, quarter)
            src_hot[q] = table
            part = dot_nn(parts[0, q], table)
            total = part if total is None else total + part
        rel_hot = hot_half(relid_ref[r], 0, rel_count)
        rel = dot_nn(rel_hi, rel_hot) + dot_nn(rel_lo, rel_hot)
        rel_rows[...] = rel
        value = total * rel
        query[...] = value
        query_half[...] = value.astype(BF)

    def edges_of(r):
        k = r + 1
        slot_ids = g * edges + lax.broadcasted_iota(jnp.int32, (1, edges), 1)
        live = jnp.where(slot_ids < counts_ref[r, 0], 1.0, 0.0)
        dst_ids = dst_ref[r]
        neg_ids = neg_ref[r]
        total = None
        for q in range(n_group):
            part = dot_nn(parts[k, q], hot_half(dst_ids, q * quarter, quarter))
            total = part if total is None else total + part
        pos = jnp.sum(query[...] * total, axis=0, keepdims=True)
        coef = -live * logistic(-pos)
        share = live * (1.0 / neg_slots)

        def one(q):
            block = parts[k, q]
            scores = dot_tn(block, query_half[...])
            base = q * quarter
            rows = lax.broadcasted_iota(jnp.int32, (quarter, neg_slots), 0) + base
            times = jnp.sum(jnp.where(rows == neg_ids, 1.0, 0.0), axis=1, keepdims=True)
            z = logistic(scores) * share * times
            z = (z + jnp.where(hot(dst_ids, base, quarter), coef, 0.0)).astype(BF)
            outbox[r, q] = dot_nt(query_half[...], z).astype(BF)
            return dot_nn(block, z)

        grad_query[...] = one(0)
        for q in range(1, n_group):
            grad_query[...] += one(q)

    def lhs_grads(r):
        term = (grad_query[...] * rel_rows[...]).astype(BF)
        for q in range(n_group):
            part = dot_nt(term, src_hot[q])
            if r == 0:
                lhs_sum[q] = part
            else:
                outbox[ROUNDS, q] = (lhs_sum[q] + part).astype(BF)

    def reduce_core(s):
        a = send(outbox.at[s, both_g], core_in.at[s, 0], (w, core_g))
        b = send(outbox.at[s, core_g], core_in.at[s, 1], (w, core_g))
        pending.extend([a, b])
        return a, b

    def reduce_pair(s, copies):
        copies[0].wait_recv()
        pair_out[s] = (outbox[s, half_g].astype(F32) + core_in[s, 0].astype(F32)).astype(BF)
        c = send(pair_out.at[s], pair_in.at[s], (w, half_g))
        copies[1].wait_recv()
        pending.append(c)
        return c

    def reduced(s, copy):
        mine = outbox[s, g].astype(F32) + core_in[s, 1].astype(F32)
        copy.wait_recv()
        return mine + pair_in[s].astype(F32)

    def give_back(s, copy):
        far_out[s] = reduced(s, copy).astype(BF)
        c = send(far_out.at[s], far_in.at[s], (dom_at(-(s + 1)), g))
        pending.append(c)
        return c

    own = forward(0, own)
    far[0].wait_recv()
    one = spread(1)
    arrived(own)
    far[1].wait_recv()
    two = spread(2)
    one = forward(1, one)
    queries(0)
    two = forward(2, two)
    arrived(one)
    edges_of(0)
    back = reduce_core(0)
    lhs_grads(0)
    back = reduce_pair(0, back)
    queries(1)
    back = give_back(0, back)
    arrived(two)
    edges_of(1)
    back_two = reduce_core(1)
    lhs_grads(1)
    lhs = reduce_core(ROUNDS)
    back_two = reduce_pair(1, back_two)
    lhs = reduce_pair(ROUNDS, lhs)
    back_two = give_back(1, back_two)
    grad = reduced(ROUNDS, lhs)
    back.wait_recv()
    grad = grad + far_in[0].astype(F32)
    back_two.wait_recv()
    grad = grad + far_in[1].astype(F32)
    new_state = state_ref[...] + jnp.sum(grad * grad, axis=0, keepdims=True) * (1.0 / width)
    new_state_ref[...] = new_state
    out_ref[...] = emb_ref[...] - grad * (LEARN_RATE / (jnp.sqrt(new_state) + ROW_EPS))
    for copy in pending:
        copy.wait_send()


def per_device(
    embeddings,
    adagrad_state,
    relation_diag,
    bucket_counts,
    src_index,
    dst_index,
    rel_index,
    neg_index,
):
    n_dom = lax.axis_size("dom")
    n_group = lax.axis_size("group")
    quarter, width = embeddings.shape
    edges = src_index.shape[2]
    neg_slots = neg_index.shape[3]
    copies = 2 + 3 * (ROUNDS + 1) + 4 * ROUNDS + 3
    vmem = pl.BlockSpec(memory_space=pltpu.VMEM)
    smem = pl.BlockSpec(memory_space=pltpu.SMEM)

    def body(*refs):
        kernel(n_dom, n_group, neg_slots, *refs)

    out, state = pl.pallas_call(
        body,
        out_shape=(
            jax.ShapeDtypeStruct((width, quarter), F32),
            jax.ShapeDtypeStruct((1, quarter), F32),
        ),
        in_specs=[smem] + [vmem] * 7,
        out_specs=(vmem, vmem),
        scratch_shapes=[
            pltpu.VMEM((ROUNDS + 1, n_group, width, quarter), BF),
            pltpu.VMEM((n_group, quarter, edges), BF),
            pltpu.VMEM((width, edges), F32),
            pltpu.VMEM((width, edges), BF),
            pltpu.VMEM((width, edges), F32),
            pltpu.VMEM((width, edges), F32),
            pltpu.VMEM((n_group, width, quarter), F32),
            pltpu.VMEM((ROUNDS + 1, n_group, width, quarter), BF),
            pltpu.VMEM((ROUNDS + 1, 2, width, quarter), BF),
            pltpu.VMEM((ROUNDS + 1, width, quarter), BF),
            pltpu.VMEM((ROUNDS + 1, width, quarter), BF),
            pltpu.VMEM((ROUNDS, width, quarter), BF),
            pltpu.VMEM((ROUNDS, width, quarter), BF),
            pltpu.SemaphoreType.DMA((copies,)),
            pltpu.SemaphoreType.DMA((copies,)),
        ],
        compiler_params=pltpu.CompilerParams(
            collective_id=0, has_side_effects=True, vmem_limit_bytes=52 * 1024 * 1024
        ),
    )(
        bucket_counts,
        embeddings.T,
        adagrad_state.reshape(1, quarter),
        relation_diag,
        src_index,
        dst_index,
        rel_index,
        neg_index.reshape(ROUNDS, 1, neg_slots),
    )
    return (out.T, state.reshape(quarter))


def solution(mesh):
    placed = (
        P(("dom", "group"), None),
        P(("dom", "group")),
        P(),
        P(None, "dom"),
        P(None, "dom", "group"),
        P(None, "dom", "group"),
        P(None, "dom", "group"),
        P(None, "dom", "group", None),
    )
    return jax.shard_map(
        per_device,
        mesh=mesh,
        in_specs=placed,
        out_specs=(P(("dom", "group"), None), P(("dom", "group"))),
        check_vma=False,
    )
```

time: 183 us -> 62.1 us (0.34)
  waiting for transfers between devices: 82.7 us -> 0 us
  Pallas kernels: 0 us -> 53.7 us
  matrix products: 36.3 us -> 0 us
  blocking collectives: 28.2 us -> 0 us
  between operations: 14.3 us -> 0.65 us
  other arithmetic: 11.2 us -> 0 us
  starting transfers between devices: 8.97 us -> 0 us
  local copies, waits for them, and re-layouts: 0.7 us -> 7.33 us
    pallas_call x0 -> x1, Pallas kernels: none -> 53.7 us  [per_device(): pl.pallas_call(body, out_shape=(jax.ShapeDtypeStruct((width, quarter), F3...]
    ppermute x4 -> x0, waiting for transfers between devices: 53 us -> none  [from_behind(): return lax.ppermute(block, axis, route)]
    dot_general x18 -> x0, matrix products: 36.3 us -> none  [the longest x4 18.5 us: add_rows(): lax.dot_general(table.astype(jnp.float32), values, (((0,), (0,)), ((), ()...]
    reduce_scatter x1 -> x0, waiting for transfers between devices: 29.7 us -> none  [per_device(): lax.psum_scatter(lhs_partial, 'group', scatter_dimension=0, tiled=True)]
    all_gather x3 -> x0, blocking collectives: 28.2 us -> none  [the longest x2 18.4 us: per_device(): rhs_block = lax.all_gather(far_quarter, 'group', axis=0, tiled=True)]
    ppermute x4 -> x0, starting transfers between devices: 8.94 us -> none  [from_behind(): return lax.ppermute(block, axis, route)]
    unnamed x18 -> x19, local copies, waits for them, and re-layouts: 0.04 us -> 7.33 us
    eq x2 -> x0, other arithmetic: 3.06 us -> none  [select_table(): return row_ids[:, None] == lax.iota(jnp.int32, count)[None, :]]
  transfers between devices with their start and end apart: 5 -> 0, of which waited for: 3 -> 0; matrix products, arithmetic and copies ran while one was open for 14% -> 0% of each run, Pallas kernels for 0% -> 0%
where the time goes in v1:
time: 62.1 us; the launch traced here: 61.7 us
  Pallas kernels  53.7 us (86%)
  local copies, waits for them, and re-layouts  7.33 us (12%)
  between operations  0.65 us (1%)
    pallas_call x1, Pallas kernels, per_device(): pl.pallas_call(body, out_shape=(jax.ShapeDtypeStruct((width, quarter), F3...  53.7 us
    unnamed x19, local copies, waits for them, and re-layouts  7.33 us

profile of v1, /device:TPU:0, one launch (start us, length us, event | category | flops | bytes accessed | tf_op | source)
XLA Modules:
  0.0 61.7 jit_solution(6573094949122004497)
XLA Ops:
  0.6 0.0 copy-start.7
  0.6 0.6 %copy-done.7 = s32[2,1]{0,1:T(1,128)S(1)} copy-done((s32[2,1]{0,1:T(1,128)S(1)}, s32[2,1]{0,1:T(1,128)}, u32[]{:S(2)}) %copy-start.7) | copy-done | bytes 32
  1.3 0.0 copy-start.6
  1.3 0.1 copy.10.refs_0_
  1.4 0.6 copy-done.6
  2.0 0.0 copy-start
  2.0 1.0 %copy-done = f32[256,400]{0,1:T(8,128)S(1)} copy-done((f32[256,400]{0,1:T(8,128)S(1)}, f32[256,400]{0,1:T(8,128)}, u32[]{:S(2)}) %copy-start) | copy-done | bytes 409624
  3.0 0.0 copy-start.1
  3.0 0.9 %copy-done.1 = f32[64,400]{1,0:T(8,128)S(1)} copy-done((f32[64,400]{1,0:T(8,128)S(1)}, f32[64,400]{1,0:T(8,128)}, u32[]{:S(2)}) %copy-start.1) | copy-done | bytes 102424
  3.9 0.0 copy-start.2
  3.9 0.7 %copy-done.2 = s32[2,1,1024]{2,1,0:T(1,128)S(1)} copy-done((s32[2,1,1024]{2,1,0:T(1,128)S(1)}, s32[2,1,1024]{2,1,0:T(1,128)}, u32[]{:S(2)}) %copy-start.2) | copy-done | bytes 8216
  4.6 0.0 copy-start.3
  4.6 0.7 %copy-done.3 = s32[2,1,1024]{2,1,0:T(1,128)S(1)} copy-done((s32[2,1,1024]{2,1,0:T(1,128)S(1)}, s32[2,1,1024]{2,1,0:T(1,128)}, u32[]{:S(2)}) %copy-start.3) | copy-done | bytes 8216
  5.3 0.0 copy-start.4
  5.3 0.7 %copy-done.4 = s32[2,1,1024]{2,1,0:T(1,128)S(1)} copy-done((s32[2,1,1024]{2,1,0:T(1,128)S(1)}, s32[2,1,1024]{2,1,0:T(1,128)}, u32[]{:S(2)}) %copy-start.4) | copy-done | bytes 8216
  6.0 0.0 copy-start.5
  6.0 0.7 %copy-done.5 = s32[2,1,1,1024]{3,2,1,0:T(1,128)S(1)} copy-done((s32[2,1,1,1024]{3,2,1,0:T(1,128)S(1)}, s32[2,1,1,1024]{3,2,1,0:T(1,128)}, u32[]{:S(2)}) %copy-start.5) | copy-done | bytes 8216
  6.7 53.7 %shard_map.95 = (f32[400,256]{1,0:T(8,128)S(1)}, f32[1,256]{1,0:T(1,128)S(1)}) custom-call(s32[2,1]{1,0:T(2,128)S(1)} %copy.10.refs_0_, f32[400,256]{1,0:T(8,128)S(1)} %bitcast.5, f32[1,256]{1,0:T(1,128)S(1)} %bitcast.8, f32[64,400]{1,0:T(8,128)S(1)} %copy-done.1, s32[2,1,1024]{2,1,0:T(1,128)S(1)} %copy-done.2, s32[2,1,1024]{2,1,0:T(1,128)S(1)} %copy-done.3, ...), custom_call_target="tpu_custom_call" | custom-call | tf_op jit(solution)/shard_map/pallas_call | solution.py:273
  60.4 0.8 %copy.13 = f32[256,400]{0,1:T(8,128)} copy(f32[256,400]{0,1:T(8,128)S(1)} %bitcast.6) | data formatting | bytes 819200
  61.2 0.6 copy.14
Async XLA Ops:
  0.6 0.7 %copy-start.7 = (s32[2,1]{0,1:T(1,128)S(1)}, s32[2,1]{0,1:T(1,128)}, u32[]{:S(2)}) copy-start(s32[2,1]{0,1:T(1,128)} %param.11) | copy-start | bytes 28
  1.3 0.7 %copy-start.6 = (f32[256]{0:T(256)S(1)}, f32[256]{0:T(256)}, u32[]{:S(2)}) copy-start(f32[256]{0:T(256)} %param.9) | copy-start | bytes 3076
  2.0 1.0 %copy-start = (f32[256,400]{0,1:T(8,128)S(1)}, f32[256,400]{0,1:T(8,128)}, u32[]{:S(2)}) copy-start(f32[256,400]{0,1:T(8,128)} %param.8) | copy-start | bytes 1228804
  3.0 0.9 %copy-start.1 = (f32[64,400]{1,0:T(8,128)S(1)}, f32[64,400]{1,0:T(8,128)}, u32[]{:S(2)}) copy-start(f32[64,400]{1,0:T(8,128)} %refs_3_.1) | copy-start | bytes 307204
  3.9 0.7 %copy-start.2 = (s32[2,1,1024]{2,1,0:T(1,128)S(1)}, s32[2,1,1024]{2,1,0:T(1,128)}, u32[]{:S(2)}) copy-start(s32[2,1,1024]{2,1,0:T(1,128)} %refs_4_.1) | copy-start | bytes 24580
  4.6 0.7 %copy-start.3 = (s32[2,1,1024]{2,1,0:T(1,128)S(1)}, s32[2,1,1024]{2,1,0:T(1,128)}, u32[]{:S(2)}) copy-start(s32[2,1,1024]{2,1,0:T(1,128)} %refs_5_.1) | copy-start | bytes 24580
  5.3 0.7 %copy-start.4 = (s32[2,1,1024]{2,1,0:T(1,128)S(1)}, s32[2,1,1024]{2,1,0:T(1,128)}, u32[]{:S(2)}) copy-start(s32[2,1,1024]{2,1,0:T(1,128)} %refs_6_.1) | copy-start | bytes 24580
  6.0 0.7 %copy-start.5 = (s32[2,1,1,1024]{3,2,1,0:T(1,128)S(1)}, s32[2,1,1,1024]{3,2,1,0:T(1,128)}, u32[]{:S(2)}) copy-start(s32[2,1,1,1024]{3,2,1,0:T(1,128)} %param.15) | copy-start | bytes 24580

commit v2 on v1

--- a/solution.py
+++ b/solution.py
@@ -34,6 +34,15 @@
     n_group,
     neg_slots,
     counts_ref,
+    emb_hbm,
+    state_hbm,
+    rel_hbm,
+    src_hbm,
+    dst_hbm,
+    relid_hbm,
+    neg_hbm,
+    out_ref,
+    new_state_ref,
     emb_ref,
     state_ref,
     rel_ref,
@@ -41,10 +50,10 @@
     dst_ref,
     relid_ref,
     neg_ref,
-    out_ref,
-    new_state_ref,
     parts,
     src_hot,
+    dst_hot,
+    times_of,
     query,
     query_half,
     rel_rows,
@@ -56,6 +65,7 @@
     pair_in,
     far_out,
     far_in,
+    load_sem,
     send_sem,
     recv_sem,
 ):
@@ -81,6 +91,14 @@
     for friend in friends:
         pl.semaphore_signal(barrier, inc=1, device_id=friend, device_id_type=MESH)
 
+    fetches = []
+    far_refs = (emb_hbm, rel_hbm, src_hbm, relid_hbm, neg_hbm, dst_hbm, state_hbm)
+    near_refs = (emb_ref, rel_ref, src_ref, relid_ref, neg_ref, dst_ref, state_ref)
+    for i, (src, dst) in enumerate(zip(far_refs, near_refs)):
+        fetch = pltpu.make_async_copy(src, dst, load_sem.at[i])
+        fetch.start()
+        fetches.append(fetch)
+    fetches[0].wait()
     parts[0, g] = emb_ref[...].astype(BF)
     pl.semaphore_wait(barrier, len(friends))
 
@@ -117,16 +135,19 @@
         for copy in copies:
             copy.wait_recv()
 
+    own = spread(0)
     far = [
         send(parts.at[0, g], parts.at[k, g], (dom_at(k), g)) for k in range(1, ROUNDS + 1)
     ]
     pending.extend(far)
-    own = spread(0)
+    for fetch in fetches[1:]:
+        fetch.wait()
 
     rel_t = rel_ref[...].T
     rel_hi = rel_t.astype(BF)
     rel_lo = (rel_t - rel_hi.astype(F32)).astype(BF)
     rel_count = rel_t.shape[1]
+    order = (both_g, core_g, half_g, g)
 
     def hot(ids, base, rows):
         return lax.broadcasted_iota(jnp.int32, (rows, edges), 0) + base == ids
@@ -134,64 +155,68 @@
     def hot_half(ids, base, rows):
         return jnp.where(hot(ids, base, rows), 1.0, 0.0).astype(BF)
 
-    def queries(r):
-        total = None
-        src_ids = src_ref[r]
+    def tables(r):
         for q in range(n_group):
-            table = hot_half(src_ids, q * quarter, quarter)
-            src_hot[q] = table
-            part = dot_nn(parts[0, q], table)
-            total = part if total is None else total + part
+            src_hot[r, q] = hot_half(src_ref[r], q * quarter, quarter)
+            dst_hot[r, q] = hot_half(dst_ref[r], q * quarter, quarter)
+            named = lax.broadcasted_iota(jnp.int32, (quarter, neg_slots), 0) + q * quarter
+            named = jnp.where(named == neg_ref[r], 1.0, 0.0)
+            times_of[r, q] = jnp.sum(named, axis=1, keepdims=True)
         rel_hot = hot_half(relid_ref[r], 0, rel_count)
-        rel = dot_nn(rel_hi, rel_hot) + dot_nn(rel_lo, rel_hot)
-        rel_rows[...] = rel
-        value = total * rel
-        query[...] = value
-        query_half[...] = value.astype(BF)
-
-    def edges_of(r):
-        k = r + 1
-        slot_ids = g * edges + lax.broadcasted_iota(jnp.int32, (1, edges), 1)
-        live = jnp.where(slot_ids < counts_ref[r, 0], 1.0, 0.0)
-        dst_ids = dst_ref[r]
-        neg_ids = neg_ref[r]
+        rel_rows[r] = dot_nn(rel_hi, rel_hot) + dot_nn(rel_lo, rel_hot)
+
+    def gathered(k, table):
         total = None
         for q in range(n_group):
-            part = dot_nn(parts[k, q], hot_half(dst_ids, q * quarter, quarter))
+            part = dot_nn(parts[k, q], table[q])
             total = part if total is None else total + part
-        pos = jnp.sum(query[...] * total, axis=0, keepdims=True)
-        coef = -live * logistic(-pos)
-        share = live * (1.0 / neg_slots)
-
-        def one(q):
-            block = parts[k, q]
-            scores = dot_tn(block, query_half[...])
-            base = q * quarter
-            rows = lax.broadcasted_iota(jnp.int32, (quarter, neg_slots), 0) + base
-            times = jnp.sum(jnp.where(rows == neg_ids, 1.0, 0.0), axis=1, keepdims=True)
-            z = logistic(scores) * share * times
-            z = (z + jnp.where(hot(dst_ids, base, quarter), coef, 0.0)).astype(BF)
-            outbox[r, q] = dot_nt(query_half[...], z).astype(BF)
-            return dot_nn(block, z)
-
-        grad_query[...] = one(0)
-        for q in range(1, n_group):
-            grad_query[...] += one(q)
+        return total
+
+    def queries(r):
+        value = gathered(0, src_hot.at[r]) * rel_rows[r]
+        query[r] = value
+        query_half[r] = value.astype(BF)
+
+    def live_of(r):
+        slot_ids = g * edges + lax.broadcasted_iota(jnp.int32, (1, edges), 1)
+        return jnp.where(slot_ids < counts_ref[0, r], 1.0, 0.0)
+
+    def coef_of(r):
+        pos = jnp.sum(query[r] * gathered(r + 1, dst_hot.at[r]), axis=0, keepdims=True)
+        return -live_of(r) * logistic(-pos)
+
+    def edges_of(r, coef):
+        share = live_of(r) * (1.0 / neg_slots)
+        copies = []
+        for i, q in enumerate(order):
+            block = parts[r + 1, q]
+            scores = dot_tn(block, query_half[r])
+            z = logistic(scores) * share * times_of[r, q]
+            z = (z + dst_hot[r, q].astype(F32) * coef).astype(BF)
+            outbox[r, q] = dot_nt(query_half[r], z).astype(BF)
+            if i < 2:
+                copies.append(send(outbox.at[r, q], core_in.at[r, i], (w, core_g)))
+            part = dot_nn(block, z)
+            if i == 0:
+                grad_query[...] = part
+            else:
+                grad_query[...] += part
+        pending.extend(copies)
+        return copies
 
     def lhs_grads(r):
-        term = (grad_query[...] * rel_rows[...]).astype(BF)
-        for q in range(n_group):
-            part = dot_nt(term, src_hot[q])
+        term = (grad_query[...] * rel_rows[r]).astype(BF)
+        copies = []
+        for i, q in enumerate(order):
+            part = dot_nt(term, src_hot[r, q])
             if r == 0:
                 lhs_sum[q] = part
-            else:
-                outbox[ROUNDS, q] = (lhs_sum[q] + part).astype(BF)
-
-    def reduce_core(s):
-        a = send(outbox.at[s, both_g], core_in.at[s, 0], (w, core_g))
-        b = send(outbox.at[s, core_g], core_in.at[s, 1], (w, core_g))
-        pending.extend([a, b])
-        return a, b
+                continue
+            outbox[ROUNDS, q] = (lhs_sum[q] + part).astype(BF)
+            if i < 2:
+                copies.append(send(outbox.at[ROUNDS, q], core_in.at[ROUNDS, i], (w, core_g)))
+        pending.extend(copies)
+        return copies
 
     def reduce_pair(s, copies):
         copies[0].wait_recv()
@@ -212,28 +237,29 @@
         pending.append(c)
         return c
 
-    own = forward(0, own)
     far[0].wait_recv()
     one = spread(1)
-    arrived(own)
+    tables(0)
+    own = forward(0, own)
     far[1].wait_recv()
     two = spread(2)
+    tables(1)
+    arrived(own)
+    queries(0)
     one = forward(1, one)
-    queries(0)
+    queries(1)
+    arrived(one)
+    coef = coef_of(0)
     two = forward(2, two)
-    arrived(one)
-    edges_of(0)
-    back = reduce_core(0)
+    back = edges_of(0, coef)
+    back = reduce_pair(0, back)
     lhs_grads(0)
-    back = reduce_pair(0, back)
-    queries(1)
+    arrived(two)
+    coef = coef_of(1)
     back = give_back(0, back)
-    arrived(two)
-    edges_of(1)
-    back_two = reduce_core(1)
-    lhs_grads(1)
-    lhs = reduce_core(ROUNDS)
+    back_two = edges_of(1, coef)
     back_two = reduce_pair(1, back_two)
+    lhs = lhs_grads(1)
     lhs = reduce_pair(ROUNDS, lhs)
     back_two = give_back(1, back_two)
     grad = reduced(ROUNDS, lhs)
@@ -276,14 +302,23 @@
             jax.ShapeDtypeStruct((width, quarter), F32),
             jax.ShapeDtypeStruct((1, quarter), F32),
         ),
-        in_specs=[smem] + [vmem] * 7,
+        in_specs=[smem] + [pl.BlockSpec(memory_space=pl.ANY)] * 7,
         out_specs=(vmem, vmem),
         scratch_shapes=[
+            pltpu.VMEM((width, quarter), F32),
+            pltpu.VMEM((1, quarter), F32),
+            pltpu.VMEM(relation_diag.shape, F32),
+            pltpu.VMEM((ROUNDS, 1, edges), jnp.int32),
+            pltpu.VMEM((ROUNDS, 1, edges), jnp.int32),
+            pltpu.VMEM((ROUNDS, 1, edges), jnp.int32),
+            pltpu.VMEM((ROUNDS, 1, neg_slots), jnp.int32),
             pltpu.VMEM((ROUNDS + 1, n_group, width, quarter), BF),
-            pltpu.VMEM((n_group, quarter, edges), BF),
-            pltpu.VMEM((width, edges), F32),
-            pltpu.VMEM((width, edges), BF),
-            pltpu.VMEM((width, edges), F32),
+            pltpu.VMEM((ROUNDS, n_group, quarter, edges), BF),
+            pltpu.VMEM((ROUNDS, n_group, quarter, edges), BF),
+            pltpu.VMEM((ROUNDS, n_group, quarter, 1), F32),
+            pltpu.VMEM((ROUNDS, width, edges), F32),
+            pltpu.VMEM((ROUNDS, width, edges), BF),
+            pltpu.VMEM((ROUNDS, width, edges), F32),
             pltpu.VMEM((width, edges), F32),
             pltpu.VMEM((n_group, width, quarter), F32),
             pltpu.VMEM((ROUNDS + 1, n_group, width, quarter), BF),
@@ -292,6 +327,7 @@
             pltpu.VMEM((ROUNDS + 1, width, quarter), BF),
             pltpu.VMEM((ROUNDS, width, quarter), BF),
             pltpu.VMEM((ROUNDS, width, quarter), BF),
+            pltpu.SemaphoreType.DMA((7,)),
             pltpu.SemaphoreType.DMA((copies,)),
             pltpu.SemaphoreType.DMA((copies,)),
         ],
@@ -299,7 +335,7 @@
             collective_id=0, has_side_effects=True, vmem_limit_bytes=52 * 1024 * 1024
         ),
     )(
-        bucket_counts,
+        bucket_counts.T,
         embeddings.T,
         adagrad_state.reshape(1, quarter),
         relation_diag,

time: 62.1 us -> 57.1 us (0.919)
  Pallas kernels: 53.7 us -> 49.4 us
  local copies, waits for them, and re-layouts: 7.33 us -> 6.67 us
    pallas_call x1, Pallas kernels: 53.7 us -> 49.4 us  [per_device(): pl.pallas_call(body, out_shape=(jax.ShapeDtypeStruct((width, quarter), F3...]
    unnamed x19 -> x18, local copies, waits for them, and re-layouts: 7.33 us -> 6.67 us
where the time goes in v2:
time: 57.1 us; the launch traced here: 56.7 us
  Pallas kernels  49.4 us (87%)
  local copies, waits for them, and re-layouts  6.67 us (12%)
  between operations  0.66 us (1%)
    pallas_call x1, Pallas kernels, per_device(): pl.pallas_call(body, out_shape=(jax.ShapeDtypeStruct((width, quarter), F3...  49.4 us
    unnamed x18, local copies, waits for them, and re-layouts  6.67 us

profile of v2, /device:TPU:0, one launch (start us, length us, event | category | flops | bytes accessed | tf_op | source)
XLA Modules:
  0.0 56.7 jit_solution(6055261803280532770)
XLA Ops:
  0.6 0.0 copy-start.6
  0.6 0.0 copy-start.7
  0.7 0.7 %copy-done.6 = f32[256]{0:T(256)S(1)} copy-done((f32[256]{0:T(256)S(1)}, f32[256]{0:T(256)}, u32[]{:S(2)}) %copy-start.6) | copy-done | bytes 1048
  1.3 0.0 copy-done.7
  1.3 0.0 copy-start
  1.3 1.0 %copy-done = f32[256,400]{0,1:T(8,128)S(1)} copy-done((f32[256,400]{0,1:T(8,128)S(1)}, f32[256,400]{0,1:T(8,128)}, u32[]{:S(2)}) %copy-start) | copy-done | bytes 409624
  2.3 0.0 copy-start.1
  2.3 0.9 %copy-done.1 = f32[64,400]{1,0:T(8,128)S(1)} copy-done((f32[64,400]{1,0:T(8,128)S(1)}, f32[64,400]{1,0:T(8,128)}, u32[]{:S(2)}) %copy-start.1) | copy-done | bytes 102424
  3.2 0.0 copy-start.2
  3.2 0.7 %copy-done.2 = s32[2,1,1024]{2,1,0:T(1,128)S(1)} copy-done((s32[2,1,1024]{2,1,0:T(1,128)S(1)}, s32[2,1,1024]{2,1,0:T(1,128)}, u32[]{:S(2)}) %copy-start.2) | copy-done | bytes 8216
  3.9 0.0 copy-start.3
  3.9 0.7 %copy-done.3 = s32[2,1,1024]{2,1,0:T(1,128)S(1)} copy-done((s32[2,1,1024]{2,1,0:T(1,128)S(1)}, s32[2,1,1024]{2,1,0:T(1,128)}, u32[]{:S(2)}) %copy-start.3) | copy-done | bytes 8216
  4.6 0.0 copy-start.4
  4.6 0.7 %copy-done.4 = s32[2,1,1024]{2,1,0:T(1,128)S(1)} copy-done((s32[2,1,1024]{2,1,0:T(1,128)S(1)}, s32[2,1,1024]{2,1,0:T(1,128)}, u32[]{:S(2)}) %copy-start.4) | copy-done | bytes 8216
  5.3 0.0 copy-start.5
  5.3 0.7 %copy-done.5 = s32[2,1,1,1024]{3,2,1,0:T(1,128)S(1)} copy-done((s32[2,1,1,1024]{3,2,1,0:T(1,128)S(1)}, s32[2,1,1,1024]{3,2,1,0:T(1,128)}, u32[]{:S(2)}) %copy-start.5) | copy-done | bytes 8216
  6.0 49.4 %shard_map.95 = (f32[400,256]{1,0:T(8,128)S(1)}, f32[1,256]{1,0:T(1,128)S(1)}) custom-call(s32[1,2]{1,0:T(1,128)S(1)} %bitcast.11, f32[400,256]{1,0:T(8,128)S(1)} %bitcast.7, f32[1,256]{1,0:T(1,128)S(1)} %bitcast.9, f32[64,400]{1,0:T(8,128)S(1)} %copy-done.1, s32[2,1,1024]{2,1,0:T(1,128)S(1)} %copy-done.2, s32[2,1,1024]{2,1,0:T(1,128)S(1)} %copy-done.3, ...), custom_call_target="tpu_custom_call" | custom-call | tf_op jit(solution)/shard_map/pallas_call | solution.py:299
  55.4 0.8 %copy.12 = f32[256,400]{0,1:T(8,128)} copy(f32[256,400]{0,1:T(8,128)S(1)} %bitcast.6) | data formatting | bytes 819200
  56.2 0.6 copy.13
Async XLA Ops:
  0.6 0.7 %copy-start.6 = (f32[256]{0:T(256)S(1)}, f32[256]{0:T(256)}, u32[]{:S(2)}) copy-start(f32[256]{0:T(256)} %param.9) | copy-start | bytes 3076
  0.6 0.7 %copy-start.7 = (s32[2,1]{0,1:T(1,128)S(1)}, s32[2,1]{0,1:T(1,128)}, u32[]{:S(2)}) copy-start(s32[2,1]{0,1:T(1,128)} %param.11) | copy-start | bytes 28
  1.3 1.0 %copy-start = (f32[256,400]{0,1:T(8,128)S(1)}, f32[256,400]{0,1:T(8,128)}, u32[]{:S(2)}) copy-start(f32[256,400]{0,1:T(8,128)} %param.8) | copy-start | bytes 1228804
  2.3 0.9 %copy-start.1 = (f32[64,400]{1,0:T(8,128)S(1)}, f32[64,400]{1,0:T(8,128)}, u32[]{:S(2)}) copy-start(f32[64,400]{1,0:T(8,128)} %refs_3_.1) | copy-start | bytes 307204
  3.2 0.7 %copy-start.2 = (s32[2,1,1024]{2,1,0:T(1,128)S(1)}, s32[2,1,1024]{2,1,0:T(1,128)}, u32[]{:S(2)}) copy-start(s32[2,1,1024]{2,1,0:T(1,128)} %refs_4_.1) | copy-start | bytes 24580
  3.9 0.7 %copy-start.3 = (s32[2,1,1024]{2,1,0:T(1,128)S(1)}, s32[2,1,1024]{2,1,0:T(1,128)}, u32[]{:S(2)}) copy-start(s32[2,1,1024]{2,1,0:T(1,128)} %refs_5_.1) | copy-start | bytes 24580
  4.6 0.7 %copy-start.4 = (s32[2,1,1024]{2,1,0:T(1,128)S(1)}, s32[2,1,1024]{2,1,0:T(1,128)}, u32[]{:S(2)}) copy-start(s32[2,1,1024]{2,1,0:T(1,128)} %refs_6_.1) | copy-start | bytes 24580
  5.3 0.7 %copy-start.5 = (s32[2,1,1,1024]{3,2,1,0:T(1,128)S(1)}, s32[2,1,1,1024]{3,2,1,0:T(1,128)}, u32[]{:S(2)}) copy-start(s32[2,1,1,1024]{3,2,1,0:T(1,128)} %param.15) | copy-start | bytes 24580
